TPU v7x, 512 devices: a whole 4x4x16 slice. The times are simulated.
512 devices in a mesh: view: 4 (over x_hi, core), brick: 128 (over z, y, x_lo).
Axes of the slice: x: 4 (x_hi: 2, x_lo: 2; x = x_hi * 2 + x_lo), y: 4, z: 16, core: 2. Of those that a mesh axis runs over, the one named last changes fastest.
Arguments:
- estimate: float32 [128, 2048, 128], P('brick'), may hold values from 0.5 to 2
- observed: float32 [4, 128, 2048, 128], P('view', None, 'brick'), may hold values from 0.25 to 4
- long_taps: float32 [4, 31], P('view'), may hold values from 0.05 to 1
- short_taps: float32 [4, 2, 7], P('view'), may hold values from 0.05 to 1
- brick_map: int32 [4, 128], P('view'), may hold values from 0 to 127, each once within a row
- valid_rows: int32 [4, 128], P('view'), may hold values from 512 to 2048
Outputs:
- refined: float32 [128, 2048, 128], P('brick')
Inputs may be any that keep to these rules, and one draw needn't show every extreme that they name: Each view's row of brick_map names every reference brick exactly once.
All inputs are finite; a program needn't handle non-finite values.
Results may differ from a plain program's by a relative error of at most 0.0001.
Values sent between devices are 32-bit elements; how exact they have to be, the bound alone decides.
A program may use at most 64 MiB of HBM per device.

v0:
```python
import jax
import jax.numpy as jnp
from jax import lax
from jax.sharding import PartitionSpec as P

ITERS = 2


def with_halo(block, sides, width):
    for axis, dim in sides:
        count = lax.axis_size(axis)
        forward = [(i, i + 1) for i in range(count - 1)]
        backward = [(target, source) for source, target in forward]
        low = lax.ppermute(
            lax.slice_in_dim(block, block.shape[dim] - width, None, axis=dim), axis, forward
        )
        high = lax.ppermute(lax.slice_in_dim(block, 0, width, axis=dim), axis, backward)
        block = jnp.concatenate([low, block, high], axis=dim)
    return block


def blur_axis(volume, kernel, dimension, adjoint):
    kernel_size = kernel.shape[0]
    radius = kernel_size // 2
    if adjoint:
        kernel = kernel[::-1]
    padding = [(0, 0)] * 3
    padding[dimension] = (radius, radius)
    padded = jnp.pad(volume, padding)
    length = volume.shape[dimension]
    summed = jnp.zeros(volume.shape, jnp.float32)
    for offset in range(kernel_size):
        summed = summed + kernel[offset] * lax.slice_in_dim(
            padded, offset, offset + length, axis=dimension
        )
    return summed


def blur_rows(volume, kernel, adjoint):
    kernel_size = kernel.shape[0]
    radius = kernel_size // 2
    if adjoint:
        kernel = kernel[::-1]
    padded = with_halo(volume, (("brick", 1),), radius)
    length = volume.shape[1]
    summed = jnp.zeros(volume.shape, jnp.float32)
    for offset in range(kernel_size):
        summed = summed + kernel[offset] * lax.slice_in_dim(padded, offset, offset + length, axis=1)
    return summed


def to_view(volume, forward_map):
    arrived = lax.all_to_all(volume, "brick", split_axis=1, concat_axis=0, tiled=True)
    brick_count = forward_map.shape[0]
    bricks = arrived.reshape(brick_count, -1, arrived.shape[1], arrived.shape[2])
    return bricks[forward_map].reshape(arrived.shape)


def to_reference(volume, inverse):
    brick_count = inverse.shape[0]
    bricks = volume.reshape(brick_count, -1, volume.shape[1], volume.shape[2])
    ordered = bricks[inverse].reshape(volume.shape)
    return lax.all_to_all(ordered, "brick", split_axis=0, concat_axis=1, tiled=True)


def on_device(estimate, observed, long_taps, short_taps, brick_map, valid_rows):
    kernel_long = long_taps[0] / jnp.sum(long_taps[0])
    kernel_plane = short_taps[0, 0] / jnp.sum(short_taps[0, 0])
    kernel_column = short_taps[0, 1] / jnp.sum(short_taps[0, 1])
    forward_map = brick_map[0]
    inverse = jnp.argsort(forward_map)
    observed_view = observed[0]
    row_count = observed_view.shape[1]
    row_ids = lax.axis_index("brick") * row_count + jnp.arange(row_count, dtype=jnp.int32)
    limits = jnp.repeat(valid_rows[0], observed_view.shape[0] // forward_map.shape[0])
    valid_mask = (row_ids[None, :] < limits[:, None])[:, :, None]
    current = estimate
    for iteration in range(ITERS):
        framed = to_view(current, forward_map)
        blurred = blur_rows(framed, kernel_long, False)
        blurred = blur_axis(blur_axis(blurred, kernel_plane, 0, False), kernel_column, 2, False)
        ratios = jnp.where(valid_mask, observed_view / blurred, 1.0)
        spread_back = blur_axis(blur_axis(ratios, kernel_plane, 0, True), kernel_column, 2, True)
        correction = to_reference(blur_rows(spread_back, kernel_long, True), inverse)
        log_terms = jnp.log(correction)
        current = current * jnp.exp(lax.psum(log_terms, "view"))
    return current


def solution(mesh):
    placed = (
        P("brick", None, None),
        P("view", None, "brick", None),
        P("view", None),
        P("view", None, None),
        P("view", None),
        P("view", None),
    )
    return jax.shard_map(
        on_device, mesh=mesh, in_specs=placed, out_specs=P("brick", None, None), check_vma=False
    )
```

profile of v0, /device:TPU:1, one launch (start us, length us, event | category | flops | bytes accessed | tf_op | source)
XLA Modules:
  0.0 746.9 jit_solution(6758244654196915608)
XLA Ops:
  6.5 21.6 %all-to-all-start = ((f32[1,2048,128]{2,0,1:T(1,128)}), f32[1,2048,128]{2,0,1:T(1,128)S(1)}, u32[]{:S(2)}, u32[]{:S(2)}) async-start(f32[1,2048,128]{2,0,1:T(1,128)} %bitcast.120), calls=%async_computation | async-start | bytes 2097152 | tf_op jit(solution)/shard_map/all_to_all | solution.py:53
  28.2 0.6 reduce_sum.27
  28.9 0.7 slice_reduce_fusion.1
  29.7 1.3 broadcast_divide_fusion.2
  31.0 0.7 fusion.367
  31.7 0.6 broadcast_divide_fusion.3
  32.3 0.7 fusion.365
  33.0 0.7 fusion.368
  33.7 43.9 %all-to-all-done = f32[1,2048,128]{2,0,1:T(1,128)S(1)} async-done(((f32[1,2048,128]{2,0,1:T(1,128)}), f32[1,2048,128]{2,0,1:T(1,128)S(1)}, u32[]{:S(2)}, u32[]{:S(2)}) %all-to-all-start) | async-done | bytes 1048608 | tf_op jit(solution)/shard_map/all_to_all | solution.py:53
  77.5 0.8 gather_fusion
  79.1 3.0 collective-permute-start
  82.1 1.3 collective-permute-start.1
  83.4 0.7 fusion.366
  84.1 0.6 broadcast_divide_fusion.4
  84.7 0.7 fusion.370
  85.5 0.7 fusion.369
  86.4 33.4 %collective-permute-done = f32[128,15,128]{2,0,1:T(8,128)S(1)} collective-permute-done((f32[128,15,128]{2,0,1:T(8,128)S(1)}, f32[128,15,128]{2,0,1:T(8,128)S(1)}, u32[]{:S(2)}, u32[]{:S(2)}) %collective-permute-start) | collective-permute-done | bytes 983072 | tf_op jit(solution)/shard_map/ppermute | solution.py:14
  119.8 0.6 copy.13
  120.4 0.6 copy_dynamic-update-slice_fusion.1
  121.0 24.0 %fusion.299 = f32[128,16,128]{2,1,0:T(8,128)S(1)} fusion(f32[128,15,128]{2,1,0:T(8,128)S(1)} %copy.13, f32[128,16,128]{2,1,0:T(8,128)S(1)} %gather_fusion, f32[128,31,128]{2,1,0:T(8,128)S(1)} %copy_dynamic-update-slice_fusion.1, f32[]{:T(128)} %bitcast.44, f32[]{:T(128)} %bitcast.43, f32[]{:T(128)} %bitcast.42, f32[]{:T(128)} %bitcast.41, f32[]{:T(128)} %bitcast.40, ...), kind=kLoop, calls=%fused_computation.495 | loop fusion | flops 19922944 | bytes 18808956 | tf_op jit(solution)/shard_map/add | solution.py:48
  145.0 4.9 multiply_add_fusion.3
  149.9 6.3 fusion.357
  156.2 4.9 multiply_add_fusion.2
  161.1 6.1 fusion.19
  167.4 1.2 copy.18
  168.6 1.3 collective-permute-start.3
  169.9 1.3 copy.16
  171.2 5.9 collective-permute-start.2
  177.2 2.6 sort.17
  179.8 0.7 fusion.364
  180.5 0.7 fusion.363
  181.2 9.6 %collective-permute-done.3 = f32[128,15,128]{2,0,1:T(8,128)} collective-permute-done((f32[128,15,128]{2,0,1:T(8,128)}, f32[128,15,128]{2,0,1:T(8,128)}, u32[]{:S(2)}, u32[]{:S(2)}) %collective-permute-start.3) | collective-permute-done | bytes 983072 | tf_op jit(solution)/shard_map/ppermute | solution.py:17
  190.8 1.8 copy.19
  192.6 26.0 %collective-permute-done.2 = f32[128,15,128]{2,0,1:T(8,128)S(1)} collective-permute-done((f32[128,15,128]{2,0,1:T(8,128)}, f32[128,15,128]{2,0,1:T(8,128)S(1)}, u32[]{:S(2)}, u32[]{:S(2)}) %collective-permute-start.2) | collective-permute-done | bytes 983072 | tf_op jit(solution)/shard_map/ppermute | solution.py:14
  218.6 0.6 copy.17
  219.1 25.1 %fusion.197 = f32[128,16,128]{2,1,0:T(8,128)S(1)} fusion(f32[128,16,128]{2,1,0:T(8,128)S(1)} %fusion.19, f32[128,15,128]{2,1,0:T(8,128)S(1)} %copy.19, f32[128,15,128]{2,1,0:T(8,128)S(1)} %copy.17, f32[]{:T(128)} %bitcast.98, f32[]{:T(128)} %bitcast.97, f32[]{:T(128)} %bitcast.96, f32[]{:T(128)} %bitcast.95, f32[]{:T(128)} %bitcast.94, f32[]{:T(128)} %bitcast.93, ...), kind=kLoop, calls=%fused_computation.393 | loop fusion | flops 23855104 | bytes 4063356 | tf_op jit(solution)/shard_map/add | solution.py:48
  244.3 0.8 gather_fusion.1
  245.1 67.0 %all_to_all.16 = f32[128,16,128]{2,1,0:T(8,128)S(1)} all-to-all(f32[128,16,128]{2,1,0:T(8,128)S(1)} %gather_fusion.1), channel_id=1, replica_groups=mesh['view'=4,'brick'=128] {'brick'}, dimensions={0} | all-to-all | bytes 2097152 | tf_op jit(solution)/shard_map/all_to_all | solution.py:63
  312.0 1.1 log.28
  313.2 58.4 %all-reduce.11.cloned.1.call-done = f32[1,2048,128]{2,1,0:T(8,128)} async-done(((f32[1,2048,128]{2,1,0:T(8,128)}), f32[1,2048,128]{2,1,0:T(8,128)}) %all-reduce.11.cloned.1.call-update) | async-done | bytes 1048592 | tf_op jit(solution)/shard_map/psum | solution.py:86
  371.6 1.4 exponential_multiply_fusion.1
  373.0 66.2 %all_to_all.17 = f32[1,2048,128]{2,0,1:T(1,128)S(1)} all-to-all(f32[1,2048,128]{2,0,1:T(1,128)S(1)} %bitcast.119), channel_id=1, replica_groups=mesh['view'=4,'brick'=128] {'brick'}, dimensions={1} | all-to-all | bytes 2097152 | tf_op jit(solution)/shard_map/all_to_all | solution.py:53
  439.2 0.8 gather_fusion.2
  440.5 2.5 collective-permute-start.4
  443.3 1.5 collective-permute-start.5
  445.0 35.9 %collective-permute-done.4 = f32[128,15,128]{2,0,1:T(8,128)S(1)} collective-permute-done((f32[128,15,128]{2,0,1:T(8,128)S(1)}, f32[128,15,128]{2,0,1:T(8,128)S(1)}, u32[]{:S(2)}, u32[]{:S(2)}) %collective-permute-start.4) | collective-permute-done | bytes 983072 | tf_op jit(solution)/shard_map/ppermute | solution.py:14
  480.9 0.6 copy.22
  481.5 0.8 collective-permute-done.5
  482.8 24.0 %fusion.155 = f32[128,16,128]{2,1,0:T(8,128)S(1)} fusion(f32[128,15,128]{2,1,0:T(8,128)S(1)} %copy.22, f32[128,16,128]{2,1,0:T(8,128)S(1)} %gather_fusion.2, f32[128,31,128]{2,1,0:T(8,128)S(1)} %copy_dynamic-update-slice_fusion, f32[]{:T(128)} %bitcast.44, f32[]{:T(128)} %bitcast.43, f32[]{:T(128)} %bitcast.42, f32[]{:T(128)} %bitcast.41, f32[]{:T(128)} %bitcast.40, ...), kind=kLoop, calls=%fused_computation.351 | loop fusion | flops 19922944 | bytes 18808956 | tf_op jit(solution)/shard_map/add | solution.py:48
  506.8 4.9 multiply_add_fusion.1
  511.7 6.3 fusion.356
  518.1 4.9 multiply_add_fusion
  522.9 6.1 fusion.44
  529.6 1.3 collective-permute-start.7
  531.2 8.0 %collective-permute-start.6 = (f32[128,15,128]{2,0,1:T(8,128)S(1)}, f32[128,15,128]{2,0,1:T(8,128)S(1)}, u32[]{:S(2)}, u32[]{:S(2)}) collective-permute-start(f32[128,15,128]{2,0,1:T(8,128)S(1)} %copy.25), channel_id=1, source_target_pairs={{0,1},{1,2},{2,3},{3,4},{4,5},{5,6},{6,7},{7,8},{8,9},{9,10},{10,1... | collective-permute-start | bytes 2949128 | tf_op jit(solution)/shard_map/ppermute | solution.py:14
  539.2 16.0 %collective-permute-done.7 = f32[128,15,128]{2,0,1:T(8,128)S(1)} collective-permute-done((f32[128,15,128]{2,0,1:T(8,128)S(1)}, f32[128,15,128]{2,0,1:T(8,128)S(1)}, u32[]{:S(2)}, u32[]{:S(2)}) %collective-permute-start.7) | collective-permute-done | bytes 983072 | tf_op jit(solution)/shard_map/ppermute | solution.py:17
  555.8 24.8 %collective-permute-done.6 = f32[128,15,128]{2,0,1:T(8,128)S(1)} collective-permute-done((f32[128,15,128]{2,0,1:T(8,128)S(1)}, f32[128,15,128]{2,0,1:T(8,128)S(1)}, u32[]{:S(2)}, u32[]{:S(2)}) %collective-permute-start.6) | collective-permute-done | bytes 983072 | tf_op jit(solution)/shard_map/ppermute | solution.py:14
  580.7 1.5 copy.26
  582.2 31.2 %fusion.53 = f32[128,16,128]{2,1,0:T(8,128)S(1)} fusion(f32[128,16,128]{2,1,0:T(8,128)S(1)} %fusion.44, f32[128,15,128]{2,1,0:T(8,128)S(1)} %copy.28, f32[128,15,128]{2,1,0:T(8,128)} %copy.26, f32[]{:T(128)} %bitcast.98, f32[]{:T(128)} %bitcast.97, f32[]{:T(128)} %bitcast.96, f32[]{:T(128)} %bitcast.95, f32[]{:T(128)} %bitcast.94, f32[]{:T(128)} %bitcast.93, ...), kind=kLoop, calls=%fused_computation.249 | loop fusion | flops 23855104 | bytes 4063356 | tf_op jit(solution)/shard_map/add | solution.py:48
  613.4 0.8 gather_fusion.3
  614.2 64.9 %all_to_all.18 = f32[128,16,128]{2,1,0:T(8,128)S(1)} all-to-all(f32[128,16,128]{2,1,0:T(8,128)S(1)} %gather_fusion.3), channel_id=1, replica_groups=mesh['view'=4,'brick'=128] {'brick'}, dimensions={0} | all-to-all | bytes 2097152 | tf_op jit(solution)/shard_map/all_to_all | solution.py:63
  679.0 1.1 log.30
  680.2 57.6 %all-reduce.13.cloned.1.call-done = f32[1,2048,128]{2,1,0:T(8,128)} async-done(((f32[1,2048,128]{2,1,0:T(8,128)}), f32[1,2048,128]{2,1,0:T(8,128)}) %all-reduce.13.cloned.1.call-update) | async-done | bytes 1048592 | tf_op jit(solution)/shard_map/psum | solution.py:86
  737.7 2.3 exponential_multiply_fusion
  (43 shorter events, 4.5 us)
Async XLA Ops:
  6.5 21.6 %copy-start.4 = (f32[1,31]{1,0:T(1,128)S(1)}, f32[1,31]{1,0:T(1,128)}, u32[]{:S(2)}) copy-start(f32[1,31]{1,0:T(1,128)} %param.8) | copy-start | bytes 376
  6.5 22.3 %copy-start.3 = (f32[1,2,7]{2,1,0:T(2,128)S(1)}, f32[1,2,7]{2,1,0:T(2,128)}, u32[]{:S(2)}) copy-start(f32[1,2,7]{2,1,0:T(2,128)} %param.9) | copy-start | bytes 172
  6.5 23.2 %copy-start.6 = (s32[1,128]{1,0:T(1,128)S(1)}, s32[1,128]{1,0:T(1,128)}, u32[]{:S(2)}) copy-start(s32[1,128]{1,0:T(1,128)} %param.10) | copy-start | bytes 1540
  6.5 71.0 %all-to-all-start = ((f32[1,2048,128]{2,0,1:T(1,128)}), f32[1,2048,128]{2,0,1:T(1,128)S(1)}, u32[]{:S(2)}, u32[]{:S(2)}) async-start(f32[1,2048,128]{2,0,1:T(1,128)} %bitcast.120), calls=%async_computation | async-start | bytes 2097152 | tf_op jit(solution)/shard_map/all_to_all | solution.py:53
  28.1 343.5 %all-reduce.11.cloned.1.call-start = ((), (), s32[]{:S(2)}) async-start(), calls=%async_computation.4 | async-start | bytes 2097152 | tf_op jit(solution)/shard_map/psum | solution.py:86
  78.4 7.8 %copy-start.5 = (s32[1,128]{1,0:T(1,128)S(1)}, s32[1,128]{1,0:T(1,128)}, u32[]{:S(2)}) copy-start(s32[1,128]{1,0:T(1,128)} %param.11) | copy-start | bytes 1540
  79.1 40.7 %collective-permute-start = (f32[128,15,128]{2,0,1:T(8,128)S(1)}, f32[128,15,128]{2,0,1:T(8,128)S(1)}, u32[]{:S(2)}, u32[]{:S(2)}) collective-permute-start(f32[128,15,128]{2,0,1:T(8,128)S(1)} %copy.12), channel_id=1, source_target_pairs={{0,1},{1,2},{2,3},{3,4},{4,5},{5,6},{6,7},{7,8},{8,9},{9,10},{10,1... | collective-permute-start | bytes 2949128 | tf_op jit(solution)/shard_map/ppermute | solution.py:14
  82.1 38.3 %collective-permute-start.1 = (f32[128,15,128]{2,0,1:T(8,128)S(1)}, f32[128,15,128]{2,0,1:T(8,128)S(1)}, u32[]{:S(2)}, u32[]{:S(2)}) collective-permute-start(f32[128,15,128]{2,0,1:T(8,128)S(1)} %copy.14), channel_id=1, source_target_pairs={{1,0},{2,1},{3,2},{4,3},{5,4},{6,5},{7,6},{8,7},{9,8},{10,9},{11,1... | collective-permute-start | bytes 2949128 | tf_op jit(solution)/shard_map/ppermute | solution.py:17
  145.0 4.9 copy-start.1
  168.6 22.1 %collective-permute-start.3 = (f32[128,15,128]{2,0,1:T(8,128)}, f32[128,15,128]{2,0,1:T(8,128)}, u32[]{:S(2)}, u32[]{:S(2)}) collective-permute-start(f32[128,15,128]{2,0,1:T(8,128)} %copy.18), channel_id=1, source_target_pairs={{1,0},{2,1},{3,2},{4,3},{5,4},{6,5},{7,6},{8,7},{9,8},{10,9},{11,1... | collective-permute-start | bytes 2949128 | tf_op jit(solution)/shard_map/ppermute | solution.py:17
  171.2 47.3 %collective-permute-start.2 = (f32[128,15,128]{2,0,1:T(8,128)}, f32[128,15,128]{2,0,1:T(8,128)S(1)}, u32[]{:S(2)}, u32[]{:S(2)}) collective-permute-start(f32[128,15,128]{2,0,1:T(8,128)} %copy.16), channel_id=1, source_target_pairs={{0,1},{1,2},{2,3},{3,4},{4,5},{5,6},{6,7},{7,8},{8,9},{9,10},{10,1... | collective-permute-start | bytes 2949128 | tf_op jit(solution)/shard_map/ppermute | solution.py:14
  312.0 59.6 %copy-start = (f32[1,2048,128]{2,1,0:T(8,128)S(1)}, f32[1,2048,128]{2,1,0:T(8,128)}, u32[]{:S(2)}) copy-start(f32[1,2048,128]{2,1,0:T(8,128)} %param.6) | copy-start | bytes 3145732
  313.2 424.6 %all-reduce.13.cloned.1.call-start = ((), (), s32[]{:S(2)}) async-start(), calls=%async_computation.5 | async-start | bytes 2097152 | tf_op jit(solution)/shard_map/psum | solution.py:86
  440.5 40.4 %collective-permute-start.4 = (f32[128,15,128]{2,0,1:T(8,128)S(1)}, f32[128,15,128]{2,0,1:T(8,128)S(1)}, u32[]{:S(2)}, u32[]{:S(2)}) collective-permute-start(f32[128,15,128]{2,0,1:T(8,128)S(1)} %copy.21), channel_id=1, source_target_pairs={{0,1},{1,2},{2,3},{3,4},{4,5},{5,6},{6,7},{7,8},{8,9},{9,10},{10,1... | collective-permute-start | bytes 2949128 | tf_op jit(solution)/shard_map/ppermute | solution.py:14
  443.3 38.9 %collective-permute-start.5 = (f32[128,15,128]{2,0,1:T(8,128)S(1)}, f32[128,15,128]{2,0,1:T(8,128)S(1)}, u32[]{:S(2)}, u32[]{:S(2)}) collective-permute-start(f32[128,15,128]{2,0,1:T(8,128)S(1)} %copy.23), channel_id=1, source_target_pairs={{1,0},{2,1},{3,2},{4,3},{5,4},{6,5},{7,6},{8,7},{9,8},{10,9},{11,1... | collective-permute-start | bytes 2949128 | tf_op jit(solution)/shard_map/ppermute | solution.py:17
  506.8 4.9 copy-start.2
  529.6 25.7 %collective-permute-start.7 = (f32[128,15,128]{2,0,1:T(8,128)S(1)}, f32[128,15,128]{2,0,1:T(8,128)S(1)}, u32[]{:S(2)}, u32[]{:S(2)}) collective-permute-start(f32[128,15,128]{2,0,1:T(8,128)S(1)} %copy.27), channel_id=1, source_target_pairs={{1,0},{2,1},{3,2},{4,3},{5,4},{6,5},{7,6},{8,7},{9,8},{10,9},{11,1... | collective-permute-start | bytes 2949128 | tf_op jit(solution)/shard_map/ppermute | solution.py:17
  531.2 49.5 %collective-permute-start.6 = (f32[128,15,128]{2,0,1:T(8,128)S(1)}, f32[128,15,128]{2,0,1:T(8,128)S(1)}, u32[]{:S(2)}, u32[]{:S(2)}) collective-permute-start(f32[128,15,128]{2,0,1:T(8,128)S(1)} %copy.25), channel_id=1, source_target_pairs={{0,1},{1,2},{2,3},{3,4},{4,5},{5,6},{6,7},{7,8},{8,9},{9,10},{10,1... | collective-permute-start | bytes 2949128 | tf_op jit(solution)/shard_map/ppermute | solution.py:14
Sparse Core Ops, SparseCore 0:
  313.3 58.3 all-reduce.10
  680.3 57.4 all-reduce.12
where the time goes:
time: 749 us; the launch traced here: 747 us
  waiting for transfers between devices  306 us (41%)
  blocking collectives  198 us (26%)
  other arithmetic  159 us (21%)
  starting transfers between devices  46.5 us (6%)
  local copies, waits for them, and re-layouts  23.3 us (3%)
  between operations  13.8 us (2%)
    all_to_all x2, blocking collectives, to_reference(): lax.all_to_all(ordered, 'brick', split_axis=0, concat_axis=1, tiled=True)  132 us
    ppermute x4, waiting for transfers between devices, with_halo(): lax.ppermute(lax.slice_in_dim(block, block.shape[dim] - width, None, axis...  120 us
    psum x2, waiting for transfers between devices, on_device(): current = current * jnp.exp(lax.psum(log_terms, 'view'))  116 us
    add x4, other arithmetic, blur_rows(): summed + kernel[offset] * lax.slice_in_dim(padded, offset, offset + lengt...  104 us
    all_to_all x1, blocking collectives, to_view(): lax.all_to_all(volume, 'brick', split_axis=1, concat_axis=0, tiled=True)  66.2 us
    all_to_all x1, waiting for transfers between devices, to_view(): lax.all_to_all(volume, 'brick', split_axis=1, concat_axis=0, tiled=True)  43.9 us
    add x6, other arithmetic, blur_axis(): summed + kernel[offset] * lax.slice_in_dim(padded, offset, offset + lengt...  31.8 us
    ppermute x4, waiting for transfers between devices, with_halo(): lax.ppermute(lax.slice_in_dim(block, 0, width, axis=dim), axis, backward)  26.4 us
  transfers between devices with their start and end apart: 11, of which 10 were waited for; matrix products, arithmetic and copies ran while one was open for 2% of the time, Pallas kernels for 0%

commit v1 on v0

--- a/solution.py
+++ b/solution.py
@@ -50,7 +50,10 @@
 
 
 def to_view(volume, forward_map):
-    arrived = lax.all_to_all(volume, "brick", split_axis=1, concat_axis=0, tiled=True)
+    n_dev = lax.axis_size("brick")
+    pieces = jnp.stack(jnp.split(volume, n_dev, axis=1), axis=0)
+    pieces = lax.all_to_all(pieces, "brick", split_axis=0, concat_axis=0)
+    arrived = jnp.concatenate(pieces, axis=0)
     brick_count = forward_map.shape[0]
     bricks = arrived.reshape(brick_count, -1, arrived.shape[1], arrived.shape[2])
     return bricks[forward_map].reshape(arrived.shape)

time: 749 us -> 929 us (1.24); the launches traced: 747 us -> 915 us
  local copies, waits for them, and re-layouts: 23.3 us -> 188 us
    unnamed x16 -> x270, local copies, waits for them, and re-layouts: 0.33 us -> 165 us
where the time goes in v1:
time: 929 us; the launch traced here: 915 us
  waiting for transfers between devices  308 us (33%)
  blocking collectives  198 us (21%)
  local copies, waits for them, and re-layouts  188 us (20%)
  other arithmetic  159 us (17%)
  starting transfers between devices  47 us (5%)
  between operations  15.3 us (2%)
    unnamed x270, local copies, waits for them, and re-layouts  165 us
    all_to_all x2, blocking collectives, to_reference(): lax.all_to_all(ordered, 'brick', split_axis=0, concat_axis=1, tiled=True)  131 us
    ppermute x4, waiting for transfers between devices, with_halo(): lax.ppermute(lax.slice_in_dim(block, block.shape[dim] - width, None, axis...  122 us
    psum x2, waiting for transfers between devices, on_device(): current = current * jnp.exp(lax.psum(log_terms, 'view'))  116 us
    add x4, other arithmetic, blur_rows(): summed + kernel[offset] * lax.slice_in_dim(padded, offset, offset + lengt...  105 us
    all_to_all x1, blocking collectives, to_view(): pieces = lax.all_to_all(pieces, 'brick', split_axis=0, concat_axis=0)  66.2 us
    all_to_all x1, waiting for transfers between devices, to_view(): pieces = lax.all_to_all(pieces, 'brick', split_axis=0, concat_axis=0)  43.9 us
    add x6, other arithmetic, blur_axis(): summed + kernel[offset] * lax.slice_in_dim(padded, offset, offset + lengt...  31.2 us
  transfers between devices with their start and end apart: 11, of which 10 were waited for; matrix products, arithmetic and copies ran while one was open for 2% of the time, Pallas kernels for 0%

profile of v1, /device:TPU:1, one launch (start us, length us, event | category | flops | bytes accessed | tf_op | source)
XLA Modules:
  0.0 915.2 jit_solution(16312308264970617379)
XLA Ops:
  6.5 1.3 constant_dynamic-update-slice_fusion.127
  7.8 1.3 constant_dynamic-update-slice_fusion.126
  9.2 1.3 constant_dynamic-update-slice_fusion.125
  11.8 1.3 constant_dynamic-update-slice_fusion.123
  13.1 1.3 constant_dynamic-update-slice_fusion.122
  14.4 1.3 constant_dynamic-update-slice_fusion.121
  15.6 1.3 constant_dynamic-update-slice_fusion.120
  16.9 1.3 constant_dynamic-update-slice_fusion.119
  19.5 1.3 constant_dynamic-update-slice_fusion.117
  20.8 1.3 constant_dynamic-update-slice_fusion.116
  22.1 1.3 constant_dynamic-update-slice_fusion.115
  23.4 1.3 constant_dynamic-update-slice_fusion.114
  24.7 1.3 constant_dynamic-update-slice_fusion.113
  26.0 1.3 constant_dynamic-update-slice_fusion.112
  27.3 1.3 constant_dynamic-update-slice_fusion.111
  28.6 1.3 constant_dynamic-update-slice_fusion.110
  29.9 1.3 constant_dynamic-update-slice_fusion.109
  32.5 1.3 constant_dynamic-update-slice_fusion.107
  33.8 1.3 constant_dynamic-update-slice_fusion.106
  35.1 1.3 constant_dynamic-update-slice_fusion.105
  36.4 1.3 constant_dynamic-update-slice_fusion.104
  37.7 1.3 constant_dynamic-update-slice_fusion.103
  40.3 1.3 constant_dynamic-update-slice_fusion.101
  41.6 1.3 constant_dynamic-update-slice_fusion.100
  42.9 1.3 constant_dynamic-update-slice_fusion.99
  44.1 1.3 constant_dynamic-update-slice_fusion.98
  45.4 1.3 constant_dynamic-update-slice_fusion.97
  48.0 1.3 constant_dynamic-update-slice_fusion.95
  49.3 1.3 constant_dynamic-update-slice_fusion.94
  172.4 21.4 %all-to-all-start = ((f32[128,1,16,128]{3,2,1,0:T(8,128)}), f32[128,1,16,128]{3,2,1,0:T(8,128)S(1)}, u32[]{:S(2)}, u32[]{:S(2)}) async-start(f32[128,1,16,128]{3,2,1,0:T(8,128)} %constant_dynamic-update-slice_fusion), calls=%async_computation | async-start | bytes 2097152 | tf_op jit(solution)/shard_map/all_to_all | solution.py:55
  199.3 43.9 %all-to-all-done = f32[128,1,16,128]{3,2,1,0:T(8,128)S(1)} async-done(((f32[128,1,16,128]{3,2,1,0:T(8,128)}), f32[128,1,16,128]{3,2,1,0:T(8,128)S(1)}, u32[]{:S(2)}, u32[]{:S(2)}) %all-to-all-start) | async-done | bytes 1048608 | tf_op jit(solution)/shard_map/all_to_all | solution.py:55
  244.8 3.0 collective-permute-start
  247.8 1.5 collective-permute-start.1
  252.3 33.3 %collective-permute-done = f32[128,15,128]{2,0,1:T(8,128)S(1)} collective-permute-done((f32[128,15,128]{2,0,1:T(8,128)S(1)}, f32[128,15,128]{2,0,1:T(8,128)S(1)}, u32[]{:S(2)}, u32[]{:S(2)}) %collective-permute-start) | collective-permute-done | bytes 983072 | tf_op jit(solution)/shard_map/ppermute | solution.py:14
  286.7 24.5 %fusion.299 = f32[128,16,128]{2,1,0:T(8,128)S(1)} fusion(f32[128,15,128]{2,1,0:T(8,128)S(1)} %copy.152, f32[128,16,128]{2,1,0:T(8,128)S(1)} %gather_fusion, f32[128,31,128]{2,1,0:T(8,128)S(1)} %copy_dynamic-update-slice_fusion.1, f32[]{:T(128)} %bitcast.171, f32[]{:T(128)} %bitcast.170, f32[]{:T(128)} %bitcast.169, f32[]{:T(128)} %bitcast.168, ...), kind=kLoop, calls=%fused_computation.495 | loop fusion | flops 19922944 | bytes 18808956 | tf_op jit(solution)/shard_map/add | solution.py:48
  311.2 5.0 multiply_add_fusion.3
  316.2 6.5 fusion.357
  322.7 4.6 multiply_add_fusion.2
  327.3 6.0 fusion.19
  336.3 6.6 collective-permute-start.2
  343.0 2.5 sort.17
  346.9 8.7 collective-permute-done.3
  356.2 27.6 %collective-permute-done.2 = f32[128,15,128]{2,0,1:T(8,128)} collective-permute-done((f32[128,15,128]{2,0,1:T(8,128)}, f32[128,15,128]{2,0,1:T(8,128)}, u32[]{:S(2)}, u32[]{:S(2)}) %collective-permute-start.2) | collective-permute-done | bytes 983072 | tf_op jit(solution)/shard_map/ppermute | solution.py:14
  383.8 1.8 copy.156
  385.6 25.0 %fusion.197 = f32[128,16,128]{2,1,0:T(8,128)S(1)} fusion(f32[128,16,128]{2,1,0:T(8,128)S(1)} %fusion.19, f32[128,15,128]{2,1,0:T(8,128)S(1)} %copy.158, f32[128,15,128]{2,1,0:T(8,128)S(1)} %copy.156, f32[]{:T(128)} %bitcast.225, f32[]{:T(128)} %bitcast.224, f32[]{:T(128)} %bitcast.223, f32[]{:T(128)} %bitcast.222, f32[]{:T(128)} %bitcast.221, f32[]{:T(128)} %bitcast.220, ...), kind=kLoop, calls=%fused_computation.393 | loop fusion | flops 23855104 | bytes 4063356 | tf_op jit(solution)/shard_map/add | solution.py:48
  411.4 66.4 %all_to_all.28 = f32[128,16,128]{2,1,0:T(8,128)S(1)} all-to-all(f32[128,16,128]{2,1,0:T(8,128)S(1)} %gather_fusion.1), channel_id=1, replica_groups=mesh['view'=4,'brick'=128] {'brick'}, dimensions={0} | all-to-all | bytes 2097152 | tf_op jit(solution)/shard_map/all_to_all | solution.py:66
  479.0 58.7 %all-reduce.11.cloned.1.call-done = f32[1,2048,128]{2,1,0:T(8,128)} async-done(((f32[1,2048,128]{2,1,0:T(8,128)}), f32[1,2048,128]{2,1,0:T(8,128)}) %all-reduce.11.cloned.1.call-update) | async-done | bytes 1048592 | tf_op jit(solution)/shard_map/psum | solution.py:89
  537.7 1.4 exponential_multiply_fusion.1
  540.5 66.2 %all_to_all.29 = f32[128,1,16,128]{3,2,1,0:T(8,128)S(1)} all-to-all(f32[128,1,16,128]{3,2,1,0:T(8,128)S(1)} %constant_dynamic-update-slice_fusion.129), channel_id=1, replica_groups=mesh['view'=4,'brick'=128] {'brick'}, dimensions={0} | all-to-all | bytes 2097152 | tf_op jit(solution)/shard_map/all_to_all | solution.py:55
  608.0 2.5 collective-permute-start.4
  612.3 36.1 %collective-permute-done.4 = f32[128,15,128]{2,0,1:T(8,128)S(1)} collective-permute-done((f32[128,15,128]{2,0,1:T(8,128)S(1)}, f32[128,15,128]{2,0,1:T(8,128)S(1)}, u32[]{:S(2)}, u32[]{:S(2)}) %collective-permute-start.4) | collective-permute-done | bytes 983072 | tf_op jit(solution)/shard_map/ppermute | solution.py:14
  650.3 24.5 %fusion.155 = f32[128,16,128]{2,1,0:T(8,128)S(1)} fusion(f32[128,15,128]{2,1,0:T(8,128)S(1)} %copy.160, f32[128,16,128]{2,1,0:T(8,128)S(1)} %gather_fusion.2, f32[128,31,128]{2,1,0:T(8,128)S(1)} %copy_dynamic-update-slice_fusion, f32[]{:T(128)} %bitcast.171, f32[]{:T(128)} %bitcast.170, f32[]{:T(128)} %bitcast.169, f32[]{:T(128)} %bitcast.168, ...), kind=kLoop, calls=%fused_computation.351 | loop fusion | flops 19922944 | bytes 18808956 | tf_op jit(solution)/shard_map/add | solution.py:48
  674.8 5.0 multiply_add_fusion.1
  679.8 6.5 fusion.356
  686.3 4.6 multiply_add_fusion
  691.0 6.0 fusion.44
  699.1 8.0 collective-permute-start.6
  707.1 16.0 %collective-permute-done.7 = f32[128,15,128]{2,0,1:T(8,128)S(1)} collective-permute-done((f32[128,15,128]{2,0,1:T(8,128)S(1)}, f32[128,15,128]{2,0,1:T(8,128)S(1)}, u32[]{:S(2)}, u32[]{:S(2)}) %collective-permute-start.7) | collective-permute-done | bytes 983072 | tf_op jit(solution)/shard_map/ppermute | solution.py:17
  723.7 24.8 %collective-permute-done.6 = f32[128,15,128]{2,0,1:T(8,128)S(1)} collective-permute-done((f32[128,15,128]{2,0,1:T(8,128)S(1)}, f32[128,15,128]{2,0,1:T(8,128)S(1)}, u32[]{:S(2)}, u32[]{:S(2)}) %collective-permute-start.6) | collective-permute-done | bytes 983072 | tf_op jit(solution)/shard_map/ppermute | solution.py:14
  748.6 1.5 copy.164
  750.1 31.2 %fusion.53 = f32[128,16,128]{2,1,0:T(8,128)S(1)} fusion(f32[128,16,128]{2,1,0:T(8,128)S(1)} %fusion.44, f32[128,15,128]{2,1,0:T(8,128)S(1)} %copy.166, f32[128,15,128]{2,1,0:T(8,128)} %copy.164, f32[]{:T(128)} %bitcast.225, f32[]{:T(128)} %bitcast.224, f32[]{:T(128)} %bitcast.223, f32[]{:T(128)} %bitcast.222, f32[]{:T(128)} %bitcast.221, f32[]{:T(128)} %bitcast.220, ...), kind=kLoop, calls=%fused_computation.249 | loop fusion | flops 23855104 | bytes 4063356 | tf_op jit(solution)/shard_map/add | solution.py:48
  782.0 64.9 %all_to_all.30 = f32[128,16,128]{2,1,0:T(8,128)S(1)} all-to-all(f32[128,16,128]{2,1,0:T(8,128)S(1)} %gather_fusion.3), channel_id=1, replica_groups=mesh['view'=4,'brick'=128] {'brick'}, dimensions={0} | all-to-all | bytes 2097152 | tf_op jit(solution)/shard_map/all_to_all | solution.py:66
  848.0 57.6 %all-reduce.13.cloned.1.call-done = f32[1,2048,128]{2,1,0:T(8,128)} async-done(((f32[1,2048,128]{2,1,0:T(8,128)}), f32[1,2048,128]{2,1,0:T(8,128)}) %all-reduce.13.cloned.1.call-update) | async-done | bytes 1048592 | tf_op jit(solution)/shard_map/psum | solution.py:89
  905.6 2.3 exponential_multiply_fusion
  (299 shorter events, 156.1 us)
Async XLA Ops:
  6.5 187.3 %copy-start.4 = (f32[1,31]{1,0:T(1,128)S(1)}, f32[1,31]{1,0:T(1,128)}, u32[]{:S(2)}) copy-start(f32[1,31]{1,0:T(1,128)} %param.8) | copy-start | bytes 376
  7.8 186.8 %copy-start.3 = (f32[1,2,7]{2,1,0:T(2,128)S(1)}, f32[1,2,7]{2,1,0:T(2,128)}, u32[]{:S(2)}) copy-start(f32[1,2,7]{2,1,0:T(2,128)} %param.9) | copy-start | bytes 172
  7.8 187.6 %copy-start.6 = (s32[1,128]{1,0:T(1,128)S(1)}, s32[1,128]{1,0:T(1,128)}, u32[]{:S(2)}) copy-start(s32[1,128]{1,0:T(1,128)} %param.10) | copy-start | bytes 1540
  172.4 70.8 %all-to-all-start = ((f32[128,1,16,128]{3,2,1,0:T(8,128)}), f32[128,1,16,128]{3,2,1,0:T(8,128)S(1)}, u32[]{:S(2)}, u32[]{:S(2)}) async-start(f32[128,1,16,128]{3,2,1,0:T(8,128)} %constant_dynamic-update-slice_fusion), calls=%async_computation | async-start | bytes 2097152 | tf_op jit(solution)/shard_map/all_to_all | solution.py:55
  193.8 343.9 %all-reduce.11.cloned.1.call-start = ((), (), s32[]{:S(2)}) async-start(), calls=%async_computation.4 | async-start | bytes 2097152 | tf_op jit(solution)/shard_map/psum | solution.py:89
  244.1 7.9 copy-start.5
  244.8 40.7 %collective-permute-start = (f32[128,15,128]{2,0,1:T(8,128)S(1)}, f32[128,15,128]{2,0,1:T(8,128)S(1)}, u32[]{:S(2)}, u32[]{:S(2)}) collective-permute-start(f32[128,15,128]{2,0,1:T(8,128)S(1)} %copy.151), channel_id=1, source_target_pairs={{0,1},{1,2},{2,3},{3,4},{4,5},{5,6},{6,7},{7,8},{8,9},{9,10},{10,1... | collective-permute-start | bytes 2949128 | tf_op jit(solution)/shard_map/ppermute | solution.py:14
  247.8 38.3 %collective-permute-start.1 = (f32[128,15,128]{2,0,1:T(8,128)S(1)}, f32[128,15,128]{2,0,1:T(8,128)S(1)}, u32[]{:S(2)}, u32[]{:S(2)}) collective-permute-start(f32[128,15,128]{2,0,1:T(8,128)S(1)} %copy.153), channel_id=1, source_target_pairs={{1,0},{2,1},{3,2},{4,3},{5,4},{6,5},{7,6},{8,7},{9,8},{10,9},{11,1... | collective-permute-start | bytes 2949128 | tf_op jit(solution)/shard_map/ppermute | solution.py:17
  311.2 5.0 copy-start.1
  333.8 21.8 %collective-permute-start.3 = (f32[128,15,128]{2,0,1:T(8,128)S(1)}, f32[128,15,128]{2,0,1:T(8,128)S(1)}, u32[]{:S(2)}, u32[]{:S(2)}) collective-permute-start(f32[128,15,128]{2,0,1:T(8,128)S(1)} %copy.157), channel_id=1, source_target_pairs={{1,0},{2,1},{3,2},{4,3},{5,4},{6,5},{7,6},{8,7},{9,8},{10,9},{11,1... | collective-permute-start | bytes 2949128 | tf_op jit(solution)/shard_map/ppermute | solution.py:17
  336.3 47.5 %collective-permute-start.2 = (f32[128,15,128]{2,0,1:T(8,128)}, f32[128,15,128]{2,0,1:T(8,128)}, u32[]{:S(2)}, u32[]{:S(2)}) collective-permute-start(f32[128,15,128]{2,0,1:T(8,128)} %copy.155), channel_id=1, source_target_pairs={{0,1},{1,2},{2,3},{3,4},{4,5},{5,6},{6,7},{7,8},{8,9},{9,10},{10,1... | collective-permute-start | bytes 2949128 | tf_op jit(solution)/shard_map/ppermute | solution.py:14
  477.8 59.9 %copy-start = (f32[1,2048,128]{2,1,0:T(8,128)S(1)}, f32[1,2048,128]{2,1,0:T(8,128)}, u32[]{:S(2)}) copy-start(f32[1,2048,128]{2,1,0:T(8,128)} %param.6) | copy-start | bytes 3145732
  479.0 426.6 %all-reduce.13.cloned.1.call-start = ((), (), s32[]{:S(2)}) async-start(), calls=%async_computation.5 | async-start | bytes 2097152 | tf_op jit(solution)/shard_map/psum | solution.py:89
  608.0 40.4 %collective-permute-start.4 = (f32[128,15,128]{2,0,1:T(8,128)S(1)}, f32[128,15,128]{2,0,1:T(8,128)S(1)}, u32[]{:S(2)}, u32[]{:S(2)}) collective-permute-start(f32[128,15,128]{2,0,1:T(8,128)S(1)} %copy.159), channel_id=1, source_target_pairs={{0,1},{1,2},{2,3},{3,4},{4,5},{5,6},{6,7},{7,8},{8,9},{9,10},{10,1... | collective-permute-start | bytes 2949128 | tf_op jit(solution)/shard_map/ppermute | solution.py:14
  610.8 38.9 %collective-permute-start.5 = (f32[128,15,128]{2,0,1:T(8,128)S(1)}, f32[128,15,128]{2,0,1:T(8,128)S(1)}, u32[]{:S(2)}, u32[]{:S(2)}) collective-permute-start(f32[128,15,128]{2,0,1:T(8,128)S(1)} %copy.161), channel_id=1, source_target_pairs={{1,0},{2,1},{3,2},{4,3},{5,4},{6,5},{7,6},{8,7},{9,8},{10,9},{11,1... | collective-permute-start | bytes 2949128 | tf_op jit(solution)/shard_map/ppermute | solution.py:17
  674.8 5.0 copy-start.2
  697.4 25.7 %collective-permute-start.7 = (f32[128,15,128]{2,0,1:T(8,128)S(1)}, f32[128,15,128]{2,0,1:T(8,128)S(1)}, u32[]{:S(2)}, u32[]{:S(2)}) collective-permute-start(f32[128,15,128]{2,0,1:T(8,128)S(1)} %copy.165), channel_id=1, source_target_pairs={{1,0},{2,1},{3,2},{4,3},{5,4},{6,5},{7,6},{8,7},{9,8},{10,9},{11,1... | collective-permute-start | bytes 2949128 | tf_op jit(solution)/shard_map/ppermute | solution.py:17
  699.1 49.5 %collective-permute-start.6 = (f32[128,15,128]{2,0,1:T(8,128)S(1)}, f32[128,15,128]{2,0,1:T(8,128)S(1)}, u32[]{:S(2)}, u32[]{:S(2)}) collective-permute-start(f32[128,15,128]{2,0,1:T(8,128)S(1)} %copy.163), channel_id=1, source_target_pairs={{0,1},{1,2},{2,3},{3,4},{4,5},{5,6},{6,7},{7,8},{8,9},{9,10},{10,1... | collective-permute-start | bytes 2949128 | tf_op jit(solution)/shard_map/ppermute | solution.py:14
Sparse Core Ops, SparseCore 0:
  479.1 58.5 all-reduce.10
  848.1 57.4 all-reduce.12
